TPU v7x, 32 devices: a whole 2x2x4 slice. The times are simulated.
32 devices in a mesh: dp: 2 (over x), fsdp: 16 (over z, y, core).
Axes of the slice: x: 2, y: 2, z: 4, core: 2. Of those that a mesh axis runs over, the one named last changes fastest.
Arguments:
- context: bfloat16 [2048, 8192], P(('dp', 'fsdp')), may hold values from -18 to 18
- residual: bfloat16 [2048, 8192], P('dp', 'fsdp'), may hold values from -45 to 45
- out_weight: bfloat16 [8192, 8192], P(None, 'fsdp'), may hold values from -0.0625 to 0.0625
- norm_gain: float32 [8192], P('fsdp'), may hold values from 0.5 to 1.5
- exit_layer: int32 [16], replicated, may hold values from 0 to 79, as said below
- destination: int32 [16], replicated, may hold values from 0 to 1, as said below
Outputs:
- hidden: bfloat16 [2048, 8192], P('dp', 'fsdp')
- normed: bfloat16 [2048, 8192], P('dp', 'fsdp')
Inputs may be any that keep to these rules, and one draw needn't show every extreme that they name: `destination`: at each position within the data groups, the destinations of the 2 passages at that position are all different. `exit_layer`: at each position i within the data groups, the passage of group i % 2 at that position is living.
All inputs are finite; a program needn't handle non-finite values.
Results may differ from a plain program's by a relative error of at most 0.0051.
Values may be sent and summed in bfloat16 or wider, within the bound.
A program may use at most 128 MiB of HBM per device.

v0:
```python
import jax
import jax.numpy as jnp
from jax import lax
from jax.sharding import PartitionSpec as P

D = 8192
LAYER = 32
PLEN = 128


def local(context, residual, out_weight, norm_gain, exit_layer, destination):
    groups = lax.axis_size("dp")
    group_index = lax.axis_index("dp")
    group_rows = residual.shape[0]
    passages = group_rows // PLEN
    living = exit_layer > LAYER
    passage_ids = group_index * passages + jnp.arange(passages, dtype=jnp.int32)
    own_living = jnp.take(living, passage_ids)
    own_target = jnp.take(destination, passage_ids)
    targets = jnp.arange(groups, dtype=jnp.int32)
    select = (own_target[None, :] == targets[:, None]) & own_living[None, :]
    row_select = jnp.repeat(select, PLEN, axis=1)
    stream = (
        jnp.dot(
            lax.all_gather(context, "fsdp", axis=0, tiled=True),
            out_weight,
            preferred_element_type=jnp.float32,
        )
        + residual.astype(jnp.float32)
    ).astype(jnp.bfloat16)
    outgoing = jnp.where(row_select[:, :, None], stream[None, :, :], jnp.zeros((), jnp.bfloat16))
    incoming = lax.all_to_all(outgoing, "dp", split_axis=0, concat_axis=0, tiled=True)
    hidden = jnp.sum(incoming, axis=0)
    hidden_wide = lax.optimization_barrier(hidden).astype(jnp.float32)
    squares = lax.psum(jnp.sum(hidden_wide * hidden_wide, axis=1), "fsdp")
    inverse_rms = lax.rsqrt(squares / D + 1e-05)
    normed = (hidden_wide * inverse_rms[:, None] * norm_gain[None, :]).astype(jnp.bfloat16)
    return (hidden, normed)


def solution(mesh):
    in_specs = (P(("dp", "fsdp"), None), P("dp", "fsdp"), P(None, "fsdp"), P("fsdp"), P(), P())
    out_specs = (P("dp", "fsdp"), P("dp", "fsdp"))
    return jax.shard_map(local, mesh=mesh, in_specs=in_specs, out_specs=out_specs, check_vma=False)
```

profile of v0, /device:TPU:0, one launch (start us, length us, event | category | flops | bytes accessed | tf_op | source)
XLA Modules:
  0.0 222.4 jit_solution(16806136172575525840)
XLA Ops:
  7.2 0.0 copy-start
  7.2 0.0 copy-start.3
  7.2 0.0 all-gather.2.cloned.1.call-start
  7.2 0.7 all-gather.2.cloned.1.call-update
  8.0 0.7 broadcast_compare_fusion
  8.6 0.6 gather_fusion.1
  9.3 0.0 copy-done
  9.3 0.6 gather_fusion
  10.0 0.1 broadcast_bitcast_fusion
  10.0 129.8 %all-gather.2.cloned.1.call-done = bf16[1024,8192]{1,0:T(8,128)(2,1)} async-done(((bf16[64,8192]{1,0:T(8,128)(2,1)}), bf16[1024,8192]{1,0:T(8,128)(2,1)}) %all-gather.2.cloned.1.call-update) | async-done | bytes 16777232 | tf_op jit(solution)/shard_map/all_gather | solution.py:25
  139.8 0.0 copy-done.3
  139.8 14.8 %add_convert_fusion = bf16[1024,512]{1,0:T(8,128)(2,1)S(1)} fusion(bf16[1024,512]{1,0:T(8,128)(2,1)S(1)} %copy-done.3, bf16[1024,8192]{1,0:T(8,128)(2,1)} %all-gather.2.cloned.1.call-done, bf16[8192,512]{1,0:T(8,128)(2,1)} %param.8), kind=kOutput, calls=%fused_computation.7 | convolution fusion | flops 8591507456 | bytes 27262976 | tf_op jit(solution)/shard_map/dot_general | solution.py:24
  154.6 0.4 broadcast_select_fusion
  155.0 28.1 %all_to_all.5 = bf16[2,1024,512]{2,1,0:T(8,128)(2,1)S(1)} all-to-all(bf16[2,1024,512]{2,1,0:T(8,128)(2,1)S(1)} %broadcast_select_fusion), channel_id=1, replica_groups=mesh['dp'=2,'fsdp'=16] {'dp'}, dimensions={0} | all-to-all | bytes 4194304 | tf_op jit(solution)/shard_map/all_to_all | solution.py:32
  183.1 0.0 copy-start.2
  183.1 1.1 reduce_sum.21
  184.2 0.0 copy-start.1
  184.2 0.3 fusion
  184.5 29.8 %psum.7 = f32[1024]{0:T(1024)S(1)} all-reduce(f32[1024]{0:T(1024)S(1)} %fusion), channel_id=1, replica_groups=mesh['dp'=2,'fsdp'=16] {'fsdp'}, use_global_device_ids=true, to_apply=%region_2.3 | all-reduce | flops 1024 | bytes 8192 | tf_op jit(solution)/shard_map/psum | solution.py:35
  214.3 0.0 copy-done.2
  214.3 1.3 fusion.2
  215.6 0.0 copy-done.1
  (7 shorter events, 0.1 us)
Async XLA Ops:
  7.2 2.1 copy-start
  7.2 132.6 %copy-start.3 = (bf16[1024,512]{1,0:T(8,128)(2,1)S(1)}, bf16[1024,512]{1,0:T(8,128)(2,1)}, u32[]{:S(2)}) copy-start(bf16[1024,512]{1,0:T(8,128)(2,1)} %param.7) | copy-start | bytes 3145732
  7.2 132.6 %all-gather.2.cloned.1.call-start = ((), (), s32[]{:S(2)}) async-start(), calls=%async_computation.1 | async-start | bytes 17825792 | tf_op jit(solution)/shard_map/all_gather | solution.py:25
  183.1 31.2 %copy-start.2 = (f32[512]{0:T(512)S(1)}, f32[512]{0:T(512)}, u32[]{:S(2)}) copy-start(f32[512]{0:T(512)} %param.9) | copy-start | bytes 6148
  184.2 31.3 %copy-start.1 = (bf16[1024,512]{1,0:T(8,128)(2,1)}, bf16[1024,512]{1,0:T(8,128)(2,1)S(1)}, u32[]{:S(2)}) copy-start(bf16[1024,512]{1,0:T(8,128)(2,1)S(1)} %reduce_sum.21) | copy-start | bytes 3145732
Sparse Core Ops, SparseCore 0:
  10.2 129.5 all-gather.1
where the time goes:
time: 223 us; the launch traced here: 222 us
  waiting for transfers between devices  130 us (58%)
  blocking collectives  57.8 us (26%)
  matrix products  14.8 us (7%)
  between operations  14.1 us (6%)
  other arithmetic  3.8 us (2%)
    all_gather x1, waiting for transfers between devices, local(): lax.all_gather(context, 'fsdp', axis=0, tiled=True)  130 us
    psum x1, blocking collectives, local(): squares = lax.psum(jnp.sum(hidden_wide * hidden_wide, axis=1), 'fsdp')  29.8 us
    all_to_all x1, blocking collectives, local(): lax.all_to_all(outgoing, 'dp', split_axis=0, concat_axis=0, tiled=True)  28.1 us
    dot_general x1, matrix products, local(): jnp.dot(lax.all_gather(context, 'fsdp', axis=0, tiled=True), out_weight,...  14.8 us
  transfers between devices with their start and end apart: 1, of which 1 were waited for; matrix products, arithmetic and copies ran while one was open for 1% of the time, Pallas kernels for 0%

commit v1 on v0

v1 whole, which is shorter than its diff:
```python
import functools

import jax
import jax.numpy as jnp
from jax import lax
from jax.experimental import pallas as pl
from jax.experimental.pallas import tpu as pltpu
from jax.sharding import PartitionSpec as P

D = 8192
LAYER = 32
PLEN = 128
LANES = 128
MESH = pl.DeviceIdType.MESH


def kernel(
    groups, members, pieces,
    context_ref, residual_ref, weight_ref, gain_ref, exit_ref, dest_ref,
    hidden_ref, normed_ref,
    ctx, weight, residual, acc, stream, incoming, hidden, normed, squares,
    ring_send, ring_recv, core_send, core_recv, own_sem, weight_sem, residual_sem,
    peer_send, peer_recv, square_send, square_recv, hidden_sem, normed_sem,
):
    rows, depth = context_ref.shape
    width = depth // pieces
    passages = residual_ref.shape[0] // PLEN
    chips = members // 2
    group = lax.axis_index("dp")
    me = lax.axis_index("fsdp")
    core = lax.rem(me, 2)
    chip = me // 2

    def chip_at(place):
        return jnp.where(place < chips // 2, 2 * place, 2 * (chips - 1 - place) + 1)

    place = jnp.where(lax.rem(chip, 2) == 0, chip // 2, chips - 1 - chip // 2)
    ahead = lax.rem(place + jnp.where(core == 0, 1, chips - 1), chips)
    target = chip_at(ahead) * 2 + core
    sibling = chip * 2 + 1 - core

    def shard_of(step, half):
        shift = chips - step if half == 0 else step
        return chip_at(lax.rem(place + shift, chips)) * 2 + half

    def ring_copy(step, piece, source=None):
        return pltpu.make_async_remote_copy(
            src_ref=ctx.at[step, piece, core] if source is None else source,
            dst_ref=ctx.at[step + 1, piece, core],
            send_sem=ring_send.at[step, piece],
            recv_sem=ring_recv.at[step + 1, piece],
            device_id=(group, target),
            device_id_type=MESH,
        )

    def core_copy(step, piece, source=None):
        return pltpu.make_async_remote_copy(
            src_ref=ctx.at[step, piece, core] if source is None else source,
            dst_ref=ctx.at[step, piece, core],
            send_sem=core_send.at[step, piece],
            recv_sem=core_recv.at[step, piece],
            device_id=(group, sibling),
            device_id_type=MESH,
        )

    def own_piece(piece):
        return context_ref.at[:, pl.ds(piece * width, width)]

    def own_copy(piece):
        return pltpu.make_async_copy(own_piece(piece), ctx.at[0, piece, core], own_sem.at[piece])

    def weight_copy(piece):
        return pltpu.make_async_copy(
            weight_ref.at[pl.ds(piece * width, width), :], weight.at[piece], weight_sem.at[piece]
        )

    residual_copy = pltpu.make_async_copy(residual_ref, residual, residual_sem)

    def peer_copy(step, distance):
        return pltpu.make_async_remote_copy(
            src_ref=stream.at[step],
            dst_ref=incoming.at[distance - 1, step],
            send_sem=peer_send.at[distance - 1, step],
            recv_sem=peer_recv.at[distance - 1, step],
            device_id=(lax.rem(group + distance, groups), me),
            device_id_type=MESH,
        )

    def square_copy(distance):
        return pltpu.make_async_remote_copy(
            src_ref=squares.at[0],
            dst_ref=squares.at[distance],
            send_sem=square_send.at[distance],
            recv_sem=square_recv.at[distance],
            device_id=(group, lax.rem(me + distance, members)),
            device_id_type=MESH,
        )

    def rows_of(shard):
        return pl.ds(pl.multiple_of(shard * rows, rows), rows)

    def hidden_copy(step, half):
        where = rows_of(shard_of(step, half))
        return pltpu.make_async_copy(
            hidden.at[where, :], hidden_ref.at[where, :], hidden_sem.at[step, half]
        )

    def normed_copy(shard):
        where = pl.ds(shard * rows, rows)
        return pltpu.make_async_copy(
            normed.at[where, :], normed_ref.at[where, :], normed_sem.at[shard]
        )

    for piece in range(pieces):
        own_copy(piece).start()
    for piece in range(pieces):
        weight_copy(piece).start()
    residual_copy.start()

    barrier = pltpu.get_barrier_semaphore()

    def greet(distance, carry):
        pl.semaphore_signal(
            barrier, inc=1, device_id=(group, lax.rem(me + distance, members)), device_id_type=MESH
        )
        return carry

    lax.fori_loop(1, members, greet, 0)
    for distance in range(1, groups):
        pl.semaphore_signal(
            barrier, inc=1, device_id=(lax.rem(group + distance, groups), me), device_id_type=MESH
        )
    pl.semaphore_wait(barrier, members - 1 + groups - 1)

    for piece in range(pieces):
        ring_copy(0, piece, own_piece(piece)).start()
        core_copy(0, piece, own_piece(piece)).start()

    def finish(step):
        for distance in range(1, groups):
            peer_copy(step, distance).wait_recv()
        total = jnp.zeros((2 * rows, LANES), jnp.float32)
        halves = []
        for half in range(2):
            shard = shard_of(step, half)
            position = shard * rows // PLEN
            chosen = None
            for distance in range(groups):
                source = lax.rem(group + groups - distance, groups)
                where = source * passages + position
                taken = jnp.logical_and(exit_ref[where] > LAYER, dest_ref[where] == group)
                block = stream[step, half] if distance == 0 else incoming[distance - 1, step, half]
                term = block.astype(jnp.float32) * taken.astype(jnp.int32).astype(jnp.float32)
                chosen = term if chosen is None else chosen + term
            hidden[rows_of(shard), :] = chosen.astype(hidden.dtype)
            hidden_copy(step, half).start()
            square = chosen * chosen
            parts = [square[:, at : at + LANES] for at in range(0, square.shape[1], LANES)]
            halves.append(functools.reduce(jnp.add, parts))
        if 2 * rows < LANES:
            halves.append(jnp.zeros((LANES - 2 * rows, LANES), jnp.float32))
        total = jnp.concatenate(halves, axis=0)
        sums = jnp.sum(total.T, axis=0, keepdims=True)
        for half in range(2):
            squares[0, pl.ds(shard_of(step, half), 1), :] = sums

    def body(turn, carry):
        @pl.when(jnp.logical_and(turn >= pieces, turn < chips * pieces))
        def _():
            step, piece = turn // pieces, lax.rem(turn, pieces)
            ring_copy(step - 1, piece).wait_recv()

            @pl.when(step < chips - 1)
            def _():
                ring_copy(step, piece).start()

            core_copy(step, piece).start()

        @pl.when(turn >= 1)
        def _():
            step, piece = (turn - 1) // pieces, lax.rem(turn - 1, pieces)

            @pl.when(step == 0)
            def _():
                own_copy(piece).wait()
                weight_copy(piece).wait()

            core_copy(step, piece).wait_recv()
            product = jnp.dot(
                ctx[step, piece].reshape(2 * rows, width),
                weight[piece],
                preferred_element_type=jnp.float32,
            )

            @pl.when(piece == 0)
            def _():
                acc[...] = product

            @pl.when(piece > 0)
            def _():
                acc[...] += product

            @pl.when(piece == pieces - 1)
            def _():
                @pl.when(step == 0)
                def _():
                    residual_copy.wait()

                for half in range(2):
                    before = residual[rows_of(shard_of(step, half)), :].astype(jnp.float32)
                    stream[step, half] = (acc[half * rows : (half + 1) * rows, :] + before).astype(
                        stream.dtype
                    )
                for distance in range(1, groups):
                    peer_copy(step, distance).start()

                @pl.when(step > 0)
                def _():
                    finish(step - 1)

        return carry

    lax.fori_loop(0, chips * pieces + 1, body, 0)
    finish(chips - 1)

    def send_squares(distance, carry):
        square_copy(distance).start()
        return carry

    def take_squares(distance, carry):
        square_copy(distance).wait_recv()
        return carry

    lax.fori_loop(1, members, send_squares, 0)
    lax.fori_loop(1, members, take_squares, 0)
    total = jnp.sum(squares[...], axis=0)
    if members < LANES:
        total = jnp.concatenate(
            [total, jnp.zeros((LANES - members, LANES), jnp.float32)], axis=0
        )
    inverse_rms = lax.rsqrt(total / D + 1e-05).T
    gain = gain_ref[...]
    for shard in range(members):
        half = shard % 2
        scale = inverse_rms[half * rows : (half + 1) * rows, shard : shard + 1]
        where = slice(shard * rows, (shard + 1) * rows)
        normed[where, :] = (hidden[where, :].astype(jnp.float32) * scale * gain).astype(normed.dtype)
        normed_copy(shard).start()

    def drain(turn, carry):
        step, piece = turn // pieces, lax.rem(turn, pieces)

        @pl.when(step < chips - 1)
        def _():
            ring_copy(step, piece).wait_send()

        core_copy(step, piece).wait_send()
        return carry

    lax.fori_loop(0, chips * pieces, drain, 0)

    def drain_steps(step, carry):
        for distance in range(1, groups):
            peer_copy(step, distance).wait_send()
        for half in range(2):
            hidden_copy(step, half).wait()
        return carry

    lax.fori_loop(0, chips, drain_steps, 0)

    def drain_squares(distance, carry):
        square_copy(distance).wait_send()
        return carry

    lax.fori_loop(1, members, drain_squares, 0)
    for shard in range(members):
        normed_copy(shard).wait()


def local(groups, members, context, residual, out_weight, norm_gain, exit_layer, destination):
    rows, depth = context.shape
    group_rows, columns = residual.shape
    chips = members // 2
    pieces = max(1, min(4, rows // 16))
    anywhere = pl.BlockSpec(memory_space=pl.ANY)
    scalars = pl.BlockSpec(memory_space=pltpu.SMEM)
    out = jax.ShapeDtypeStruct((group_rows, columns), jnp.bfloat16)
    dma = pltpu.SemaphoreType.DMA
    return pl.pallas_call(
        functools.partial(kernel, groups, members, pieces),
        out_shape=(out, out),
        in_specs=[anywhere, anywhere, anywhere, pl.BlockSpec(memory_space=pltpu.VMEM), scalars, scalars],
        out_specs=(anywhere, anywhere),
        scratch_shapes=[
            pltpu.VMEM((chips, pieces, 2, rows, depth // pieces), jnp.bfloat16),
            pltpu.VMEM((pieces, depth // pieces, columns), jnp.bfloat16),
            pltpu.VMEM((group_rows, columns), jnp.bfloat16),
            pltpu.VMEM((2 * rows, columns), jnp.float32),
            pltpu.VMEM((chips, 2, rows, columns), jnp.bfloat16),
            pltpu.VMEM((groups - 1, chips, 2, rows, columns), jnp.bfloat16),
            pltpu.VMEM((group_rows, columns), jnp.bfloat16),
            pltpu.VMEM((group_rows, columns), jnp.bfloat16),
            pltpu.VMEM((members, members, LANES), jnp.float32),
            dma((chips, pieces)),
            dma((chips, pieces)),
            dma((chips, pieces)),
            dma((chips, pieces)),
            dma((pieces,)),
            dma((pieces,)),
            dma(()),
            dma((groups - 1, chips)),
            dma((groups - 1, chips)),
            dma((members,)),
            dma((members,)),
            dma((chips, 2)),
            dma((members,)),
        ],
        compiler_params=pltpu.CompilerParams(
            collective_id=0, has_side_effects=True, vmem_limit_bytes=52 * 1024 * 1024
        ),
        cost_estimate=pl.CostEstimate(
            flops=2 * group_rows * depth * columns,
            bytes_accessed=2 * (rows * depth + depth * columns + 3 * group_rows * columns),
            transcendentals=0,
        ),
    )(context, residual, out_weight, norm_gain.reshape(1, columns), exit_layer, destination)


def solution(mesh):
    in_specs = (P(("dp", "fsdp"), None), P("dp", "fsdp"), P(None, "fsdp"), P("fsdp"), P(), P())
    out_specs = (P("dp", "fsdp"), P("dp", "fsdp"))
    body = functools.partial(local, mesh.shape["dp"], mesh.shape["fsdp"])
    return jax.shard_map(body, mesh=mesh, in_specs=in_specs, out_specs=out_specs, check_vma=False)
```

time: 223 us -> 108 us (0.48)
  waiting for transfers between devices: 130 us -> 0 us
  Pallas kernels: 0 us -> 102 us
  blocking collectives: 57.8 us -> 0 us
  matrix products: 14.8 us -> 0 us
  between operations: 14.1 us -> 0.65 us
  local copies, waits for them, and re-layouts: 1.4 us -> 5.22 us
  other arithmetic: 3.8 us -> 0 us
    all_gather x1 -> x0, waiting for transfers between devices: 130 us -> none  [local(): lax.all_gather(context, 'fsdp', axis=0, tiled=True)]
    pallas_call x0 -> x1, Pallas kernels: none -> 102 us  [local(): pl.pallas_call(functools.partial(kernel, groups, members, pieces), out_sh...]
    psum x1 -> x0, blocking collectives: 29.8 us -> none  [local(): squares = lax.psum(jnp.sum(hidden_wide * hidden_wide, axis=1), 'fsdp')]
    all_to_all x1 -> x0, blocking collectives: 28.1 us -> none  [local(): lax.all_to_all(outgoing, 'dp', split_axis=0, concat_axis=0, tiled=True)]
    dot_general x1 -> x0, matrix products: 14.8 us -> none  [local(): jnp.dot(lax.all_gather(context, 'fsdp', axis=0, tiled=True), out_weight,...]
    unnamed x10 -> x8, local copies, waits for them, and re-layouts: 0.11 us -> 5.22 us
  transfers between devices with their start and end apart: 1 -> 0, of which waited for: 1 -> 0; matrix products, arithmetic and copies ran while one was open for 1% -> 0% of each run, Pallas kernels for 0% -> 0%
where the time goes in v1:
time: 108 us
  Pallas kernels  102 us (94%)
  local copies, waits for them, and re-layouts  5.22 us (5%)
    pallas_call x1, Pallas kernels, local(): pl.pallas_call(functools.partial(kernel, groups, members, pieces), out_sh...  102 us
    unnamed x8, local copies, waits for them, and re-layouts  5.22 us

profile of v1, /device:TPU:0, one launch (start us, length us, event | category | flops | bytes accessed | tf_op | source)
XLA Modules:
  0.0 107.6 jit_solution(9854950015775970095)
XLA Ops:
  0.6 0.0 copy-start
  0.6 0.7 copy-done
  1.3 0.0 copy-start.1
  1.3 0.7 copy-done.1
  2.0 0.0 copy-start.2
  2.0 0.7 copy-done.2
  2.6 101.7 %shard_map.77 = (bf16[1024,512]{1,0:T(8,128)(2,1)S(1)}, bf16[1024,512]{1,0:T(8,128)(2,1)}) custom-call(bf16[64,8192]{1,0:T(8,128)(2,1)} %context_ref.1, bf16[1024,512]{1,0:T(8,128)(2,1)} %residual_ref.1, bf16[8192,512]{1,0:T(8,128)(2,1)} %weight_ref.1, f32[1,512]{1,0:T(1,128)S(1)} %bitcast.1, s32[16]{0:T(128)S(1)} %copy-done.1, s32[16]{0:T(128)S(1)} %copy-done.2), custom_call_target="tpu_custom_call" | custom-call | flops 8589934592 | bytes 12582912 | tf_op jit(solution)/shard_map/pallas_call | solution.py:289
  104.3 1.0 copy.10
  105.3 2.3 %copy.11 = bf16[1024,512]{1,0:T(8,128)(2,1)} copy(bf16[1024,512]{1,0:T(8,128)(2,1)} %get-tuple-element.5) | data formatting | bytes 2097152
Async XLA Ops:
  0.6 0.7 copy-start
  1.3 0.7 copy-start.1
  2.0 0.7 copy-start.2

commit v2 on v1

--- a/solution.py
+++ b/solution.py
@@ -17,10 +17,10 @@
 def kernel(
     groups, members, pieces,
     context_ref, residual_ref, weight_ref, gain_ref, exit_ref, dest_ref,
-    hidden_ref, normed_ref,
-    ctx, weight, residual, acc, stream, incoming, hidden, normed, squares,
+    hidden, normed,
+    ctx, weight, residual, acc, stream, incoming, squares,
     ring_send, ring_recv, core_send, core_recv, own_sem, weight_sem, residual_sem,
-    peer_send, peer_recv, square_send, square_recv, hidden_sem, normed_sem,
+    peer_send, peer_recv, square_send, square_recv,
 ):
     rows, depth = context_ref.shape
     width = depth // pieces
@@ -99,38 +99,23 @@
     def rows_of(shard):
         return pl.ds(pl.multiple_of(shard * rows, rows), rows)
 
-    def hidden_copy(step, half):
-        where = rows_of(shard_of(step, half))
-        return pltpu.make_async_copy(
-            hidden.at[where, :], hidden_ref.at[where, :], hidden_sem.at[step, half]
-        )
-
-    def normed_copy(shard):
-        where = pl.ds(shard * rows, rows)
-        return pltpu.make_async_copy(
-            normed.at[where, :], normed_ref.at[where, :], normed_sem.at[shard]
-        )
-
     for piece in range(pieces):
         own_copy(piece).start()
     for piece in range(pieces):
         weight_copy(piece).start()
     residual_copy.start()
+    squares[0] = jnp.zeros(squares.shape[1:], jnp.float32)
 
     barrier = pltpu.get_barrier_semaphore()
 
-    def greet(distance, carry):
-        pl.semaphore_signal(
-            barrier, inc=1, device_id=(group, lax.rem(me + distance, members)), device_id_type=MESH
-        )
-        return carry
-
-    lax.fori_loop(1, members, greet, 0)
+    behind = lax.rem(place + jnp.where(core == 0, chips - 1, 1), chips)
+    for member in (target, chip_at(behind) * 2 + core, sibling):
+        pl.semaphore_signal(barrier, inc=1, device_id=(group, member), device_id_type=MESH)
     for distance in range(1, groups):
         pl.semaphore_signal(
             barrier, inc=1, device_id=(lax.rem(group + distance, groups), me), device_id_type=MESH
         )
-    pl.semaphore_wait(barrier, members - 1 + groups - 1)
+    pl.semaphore_wait(barrier, 3 + groups - 1)
 
     for piece in range(pieces):
         ring_copy(0, piece, own_piece(piece)).start()
@@ -139,7 +124,6 @@
     def finish(step):
         for distance in range(1, groups):
             peer_copy(step, distance).wait_recv()
-        total = jnp.zeros((2 * rows, LANES), jnp.float32)
         halves = []
         for half in range(2):
             shard = shard_of(step, half)
@@ -153,7 +137,6 @@
                 term = block.astype(jnp.float32) * taken.astype(jnp.int32).astype(jnp.float32)
                 chosen = term if chosen is None else chosen + term
             hidden[rows_of(shard), :] = chosen.astype(hidden.dtype)
-            hidden_copy(step, half).start()
             square = chosen * chosen
             parts = [square[:, at : at + LANES] for at in range(0, square.shape[1], LANES)]
             halves.append(functools.reduce(jnp.add, parts))
@@ -161,8 +144,10 @@
             halves.append(jnp.zeros((LANES - 2 * rows, LANES), jnp.float32))
         total = jnp.concatenate(halves, axis=0)
         sums = jnp.sum(total.T, axis=0, keepdims=True)
+        lane = lax.broadcasted_iota(jnp.int32, sums.shape, 1)
         for half in range(2):
-            squares[0, pl.ds(shard_of(step, half), 1), :] = sums
+            own = jnp.logical_and(lane >= half * rows, lane < (half + 1) * rows)
+            squares[0, pl.ds(shard_of(step, half) // 2, 1), :] += jnp.where(own, sums, 0.0)
 
     def body(turn, carry):
         @pl.when(jnp.logical_and(turn >= pieces, turn < chips * pieces))
@@ -234,18 +219,17 @@
     lax.fori_loop(1, members, send_squares, 0)
     lax.fori_loop(1, members, take_squares, 0)
     total = jnp.sum(squares[...], axis=0)
-    if members < LANES:
+    if chips < LANES:
         total = jnp.concatenate(
-            [total, jnp.zeros((LANES - members, LANES), jnp.float32)], axis=0
+            [total, jnp.zeros((LANES - chips, LANES), jnp.float32)], axis=0
         )
     inverse_rms = lax.rsqrt(total / D + 1e-05).T
     gain = gain_ref[...]
     for shard in range(members):
         half = shard % 2
-        scale = inverse_rms[half * rows : (half + 1) * rows, shard : shard + 1]
+        scale = inverse_rms[half * rows : (half + 1) * rows, shard // 2 : shard // 2 + 1]
         where = slice(shard * rows, (shard + 1) * rows)
         normed[where, :] = (hidden[where, :].astype(jnp.float32) * scale * gain).astype(normed.dtype)
-        normed_copy(shard).start()
 
     def drain(turn, carry):
         step, piece = turn // pieces, lax.rem(turn, pieces)
@@ -262,8 +246,6 @@
     def drain_steps(step, carry):
         for distance in range(1, groups):
             peer_copy(step, distance).wait_send()
-        for half in range(2):
-            hidden_copy(step, half).wait()
         return carry
 
     lax.fori_loop(0, chips, drain_steps, 0)
@@ -273,8 +255,6 @@
         return carry
 
     lax.fori_loop(1, members, drain_squares, 0)
-    for shard in range(members):
-        normed_copy(shard).wait()
 
 
 def local(groups, members, context, residual, out_weight, norm_gain, exit_layer, destination):
@@ -290,7 +270,7 @@
         functools.partial(kernel, groups, members, pieces),
         out_shape=(out, out),
         in_specs=[anywhere, anywhere, anywhere, pl.BlockSpec(memory_space=pltpu.VMEM), scalars, scalars],
-        out_specs=(anywhere, anywhere),
+        out_specs=(pl.BlockSpec(memory_space=pltpu.VMEM),) * 2,
         scratch_shapes=[
             pltpu.VMEM((chips, pieces, 2, rows, depth // pieces), jnp.bfloat16),
             pltpu.VMEM((pieces, depth // pieces, columns), jnp.bfloat16),
@@ -298,9 +278,7 @@
             pltpu.VMEM((2 * rows, columns), jnp.float32),
             pltpu.VMEM((chips, 2, rows, columns), jnp.bfloat16),
             pltpu.VMEM((groups - 1, chips, 2, rows, columns), jnp.bfloat16),
-            pltpu.VMEM((group_rows, columns), jnp.bfloat16),
-            pltpu.VMEM((group_rows, columns), jnp.bfloat16),
-            pltpu.VMEM((members, members, LANES), jnp.float32),
+            pltpu.VMEM((members, chips, LANES), jnp.float32),
             dma((chips, pieces)),
             dma((chips, pieces)),
             dma((chips, pieces)),
@@ -312,11 +290,9 @@
             dma((groups - 1, chips)),
             dma((members,)),
             dma((members,)),
-            dma((chips, 2)),
-            dma((members,)),
         ],
         compiler_params=pltpu.CompilerParams(
-            collective_id=0, has_side_effects=True, vmem_limit_bytes=52 * 1024 * 1024
+            collective_id=0, has_side_effects=True, vmem_limit_bytes=51 * 1024 * 1024
         ),
         cost_estimate=pl.CostEstimate(
             flops=2 * group_rows * depth * columns,

time: 108 us -> 105 us (0.972)
  Pallas kernels: 102 us -> 100 us
  local copies, waits for them, and re-layouts: 5.22 us -> 3.93 us
    pallas_call x1, Pallas kernels: 102 us -> 100 us  [local(): pl.pallas_call(functools.partial(kernel, groups, members, pieces), out_sh...]
    unnamed x8, local copies, waits for them, and re-layouts: 5.22 us -> 3.93 us
where the time goes in v2:
time: 105 us
  Pallas kernels  100 us (95%)
  local copies, waits for them, and re-layouts  3.93 us (4%)
    pallas_call x1, Pallas kernels, local(): pl.pallas_call(functools.partial(kernel, groups, members, pieces), out_sh...  100 us
    unnamed x8, local copies, waits for them, and re-layouts  3.93 us

profile of v2, /device:TPU:0, one launch (start us, length us, event | category | flops | bytes accessed | tf_op | source)
XLA Modules:
  0.0 104.6 jit_solution(13707055618269524562)
XLA Ops:
  0.6 0.0 copy-start
  0.6 0.7 copy-done
  1.3 0.0 copy-start.1
  1.3 0.7 copy-done.1
  2.0 0.0 copy-start.2
  2.0 0.7 copy-done.2
  2.6 100.0 %shard_map.77 = (bf16[1024,512]{1,0:T(8,128)(2,1)S(1)}, bf16[1024,512]{1,0:T(8,128)(2,1)S(1)}) custom-call(bf16[64,8192]{1,0:T(8,128)(2,1)} %context_ref.1, bf16[1024,512]{1,0:T(8,128)(2,1)} %residual_ref.1, bf16[8192,512]{1,0:T(8,128)(2,1)} %weight_ref.1, f32[1,512]{1,0:T(1,128)S(1)} %bitcast.1, s32[16]{0:T(128)S(1)} %copy-done.1, s32[16]{0:T(128)S(1)} %copy-done.2), custom_call_target="tpu_custom_call" | custom-call | flops 8589934592 | bytes 12582912 | tf_op jit(solution)/shard_map/pallas_call | solution.py:269
  102.6 1.0 copy.10
  103.6 1.0 copy.11
Async XLA Ops:
  0.6 0.7 copy-start
  1.3 0.7 copy-start.1
  2.0 0.7 copy-start.2

commit v3 on v2

--- a/solution.py
+++ b/solution.py
@@ -86,15 +86,23 @@
             device_id_type=MESH,
         )
 
-    def square_copy(distance):
+    def square_copy(index):
         return pltpu.make_async_remote_copy(
             src_ref=squares.at[0],
-            dst_ref=squares.at[distance],
-            send_sem=square_send.at[distance],
-            recv_sem=square_recv.at[distance],
-            device_id=(group, lax.rem(me + distance, members)),
+            dst_ref=squares.at[index],
+            send_sem=square_send.at[index],
+            recv_sem=square_recv.at[index],
+            device_id=(
+                lax.rem(group + index // members, groups),
+                lax.rem(me + lax.rem(index, members), members),
+            ),
             device_id_type=MESH,
         )
+
+    def taken_of(shard, distance):
+        where = lax.rem(group + groups - distance, groups) * passages + shard * rows // PLEN
+        taken = jnp.logical_and(exit_ref[where] > LAYER, dest_ref[where] == group)
+        return taken.astype(jnp.int32).astype(jnp.float32)
 
     def rows_of(shard):
         return pl.ds(pl.multiple_of(shard * rows, rows), rows)
@@ -121,33 +129,31 @@
         ring_copy(0, piece, own_piece(piece)).start()
         core_copy(0, piece, own_piece(piece)).start()
 
-    def finish(step):
-        for distance in range(1, groups):
-            peer_copy(step, distance).wait_recv()
+    def add_squares(step, blocks):
         halves = []
-        for half in range(2):
-            shard = shard_of(step, half)
-            position = shard * rows // PLEN
-            chosen = None
-            for distance in range(groups):
-                source = lax.rem(group + groups - distance, groups)
-                where = source * passages + position
-                taken = jnp.logical_and(exit_ref[where] > LAYER, dest_ref[where] == group)
-                block = stream[step, half] if distance == 0 else incoming[distance - 1, step, half]
-                term = block.astype(jnp.float32) * taken.astype(jnp.int32).astype(jnp.float32)
-                chosen = term if chosen is None else chosen + term
-            hidden[rows_of(shard), :] = chosen.astype(hidden.dtype)
-            square = chosen * chosen
+        for block in blocks:
+            square = block * block
             parts = [square[:, at : at + LANES] for at in range(0, square.shape[1], LANES)]
             halves.append(functools.reduce(jnp.add, parts))
         if 2 * rows < LANES:
             halves.append(jnp.zeros((LANES - 2 * rows, LANES), jnp.float32))
-        total = jnp.concatenate(halves, axis=0)
-        sums = jnp.sum(total.T, axis=0, keepdims=True)
+        sums = jnp.sum(jnp.concatenate(halves, axis=0).T, axis=0, keepdims=True)
         lane = lax.broadcasted_iota(jnp.int32, sums.shape, 1)
         for half in range(2):
             own = jnp.logical_and(lane >= half * rows, lane < (half + 1) * rows)
             squares[0, pl.ds(shard_of(step, half) // 2, 1), :] += jnp.where(own, sums, 0.0)
+
+    def finish(step):
+        for distance in range(1, groups):
+            peer_copy(step, distance).wait_recv()
+        for half in range(2):
+            shard = shard_of(step, half)
+            chosen = None
+            for distance in range(groups):
+                block = stream[step, half] if distance == 0 else incoming[distance - 1, step, half]
+                term = block.astype(jnp.float32) * taken_of(shard, distance)
+                chosen = term if chosen is None else chosen + term
+            hidden[rows_of(shard), :] = chosen.astype(hidden.dtype)
 
     def body(turn, carry):
         @pl.when(jnp.logical_and(turn >= pieces, turn < chips * pieces))
@@ -191,43 +197,53 @@
                 def _():
                     residual_copy.wait()
 
+                blocks = []
                 for half in range(2):
                     before = residual[rows_of(shard_of(step, half)), :].astype(jnp.float32)
-                    stream[step, half] = (acc[half * rows : (half + 1) * rows, :] + before).astype(
-                        stream.dtype
-                    )
+                    block = (acc[half * rows : (half + 1) * rows, :] + before).astype(stream.dtype)
+                    stream[step, half] = block
+                    blocks.append(block.astype(jnp.float32))
                 for distance in range(1, groups):
                     peer_copy(step, distance).start()
 
-                @pl.when(step > 0)
+                add_squares(step, blocks)
+
+                @pl.when(jnp.logical_and(step > 0, step < chips - 1))
                 def _():
                     finish(step - 1)
 
         return carry
 
     lax.fori_loop(0, chips * pieces + 1, body, 0)
+
+    def send_squares(index, carry):
+        square_copy(index).start()
+        return carry
+
+    def take_squares(index, carry):
+        square_copy(index).wait_recv()
+        return carry
+
+    lax.fori_loop(1, groups * members, send_squares, 0)
+    finish(chips - 2)
     finish(chips - 1)
-
-    def send_squares(distance, carry):
-        square_copy(distance).start()
-        return carry
-
-    def take_squares(distance, carry):
-        square_copy(distance).wait_recv()
-        return carry
-
-    lax.fori_loop(1, members, send_squares, 0)
-    lax.fori_loop(1, members, take_squares, 0)
-    total = jnp.sum(squares[...], axis=0)
-    if chips < LANES:
-        total = jnp.concatenate(
-            [total, jnp.zeros((LANES - chips, LANES), jnp.float32)], axis=0
-        )
-    inverse_rms = lax.rsqrt(total / D + 1e-05).T
+    lax.fori_loop(1, groups * members, take_squares, 0)
+    inverse_rms = []
+    for distance in range(groups):
+        total = jnp.sum(squares[distance * members : (distance + 1) * members], axis=0)
+        if chips < LANES:
+            total = jnp.concatenate(
+                [total, jnp.zeros((LANES - chips, LANES), jnp.float32)], axis=0
+            )
+        inverse_rms.append(lax.rsqrt(total / D + 1e-05).T)
     gain = gain_ref[...]
     for shard in range(members):
         half = shard % 2
-        scale = inverse_rms[half * rows : (half + 1) * rows, shard // 2 : shard // 2 + 1]
+        scale = sum(
+            inverse[half * rows : (half + 1) * rows, shard // 2 : shard // 2 + 1]
+            * taken_of(shard, distance)
+            for distance, inverse in enumerate(inverse_rms)
+        )
         where = slice(shard * rows, (shard + 1) * rows)
         normed[where, :] = (hidden[where, :].astype(jnp.float32) * scale * gain).astype(normed.dtype)
 
@@ -254,7 +270,7 @@
         square_copy(distance).wait_send()
         return carry
 
-    lax.fori_loop(1, members, drain_squares, 0)
+    lax.fori_loop(1, groups * members, drain_squares, 0)
 
 
 def local(groups, members, context, residual, out_weight, norm_gain, exit_layer, destination):
@@ -278,7 +294,7 @@
             pltpu.VMEM((2 * rows, columns), jnp.float32),
             pltpu.VMEM((chips, 2, rows, columns), jnp.bfloat16),
             pltpu.VMEM((groups - 1, chips, 2, rows, columns), jnp.bfloat16),
-            pltpu.VMEM((members, chips, LANES), jnp.float32),
+            pltpu.VMEM((groups * members, chips, LANES), jnp.float32),
             dma((chips, pieces)),
             dma((chips, pieces)),
             dma((chips, pieces)),
@@ -288,8 +304,8 @@
             dma(()),
             dma((groups - 1, chips)),
             dma((groups - 1, chips)),
-            dma((members,)),
-            dma((members,)),
+            dma((groups * members,)),
+            dma((groups * members,)),
         ],
         compiler_params=pltpu.CompilerParams(
             collective_id=0, has_side_effects=True, vmem_limit_bytes=51 * 1024 * 1024

time: 105 us -> 103 us (0.981)
  Pallas kernels: 100 us -> 97.8 us
    pallas_call x1, Pallas kernels: 100 us -> 97.8 us  [local(): pl.pallas_call(functools.partial(kernel, groups, members, pieces), out_sh...]
where the time goes in v3:
time: 103 us; the launch traced here: 102 us
  Pallas kernels  97.8 us (95%)
  local copies, waits for them, and re-layouts  3.93 us (4%)
    pallas_call x1, Pallas kernels, local(): pl.pallas_call(functools.partial(kernel, groups, members, pieces), out_sh...  97.8 us
    unnamed x8, local copies, waits for them, and re-layouts  3.93 us

profile of v3, /device:TPU:0, one launch (start us, length us, event | category | flops | bytes accessed | tf_op | source)
XLA Modules:
  0.0 102.4 jit_solution(11366179486170644223)
XLA Ops:
  0.6 0.0 copy-start
  0.6 0.7 copy-done
  1.3 0.0 copy-start.1
  1.3 0.7 copy-done.1
  2.0 0.0 copy-start.2
  2.0 0.7 copy-done.2
  2.6 97.8 %shard_map.77 = (bf16[1024,512]{1,0:T(8,128)(2,1)S(1)}, bf16[1024,512]{1,0:T(8,128)(2,1)S(1)}) custom-call(bf16[64,8192]{1,0:T(8,128)(2,1)} %context_ref.1, bf16[1024,512]{1,0:T(8,128)(2,1)} %residual_ref.1, bf16[8192,512]{1,0:T(8,128)(2,1)} %weight_ref.1, f32[1,512]{1,0:T(1,128)S(1)} %bitcast.1, s32[16]{0:T(128)S(1)} %copy-done.1, s32[16]{0:T(128)S(1)} %copy-done.2), custom_call_target="tpu_custom_call" | custom-call | flops 8589934592 | bytes 12582912 | tf_op jit(solution)/shard_map/pallas_call | solution.py:285
  100.4 1.0 copy.10
  101.4 1.0 copy.11
Async XLA Ops:
  0.6 0.7 copy-start
  1.3 0.7 copy-start.1
  2.0 0.7 copy-start.2

commit v4 on v3

--- a/solution.py
+++ b/solution.py
@@ -127,6 +127,7 @@
 
     for piece in range(pieces):
         ring_copy(0, piece, own_piece(piece)).start()
+    for piece in range(pieces):
         core_copy(0, piece, own_piece(piece)).start()
 
     def add_squares(step, blocks):
@@ -217,7 +218,7 @@
     lax.fori_loop(0, chips * pieces + 1, body, 0)
 
     def send_squares(index, carry):
-        square_copy(index).start()
+        square_copy(groups * members - index).start()
         return carry
 
     def take_squares(index, carry):

time: 103 us -> 103 us (level)
  no operation moved by 1% of the time
where the time goes in v4:
time: 103 us; the launch traced here: 102 us
  Pallas kernels  97.8 us (95%)
  local copies, waits for them, and re-layouts  3.93 us (4%)
    pallas_call x1, Pallas kernels, local(): pl.pallas_call(functools.partial(kernel, groups, members, pieces), out_sh...  97.8 us
    unnamed x8, local copies, waits for them, and re-layouts  3.93 us

profile of v4, /device:TPU:0, one launch (start us, length us, event | category | flops | bytes accessed | tf_op | source)
XLA Modules:
  0.0 102.4 jit_solution(2729777923448665412)
XLA Ops:
  0.6 0.0 copy-start
  0.6 0.7 copy-done
  1.3 0.0 copy-start.1
  1.3 0.7 copy-done.1
  2.0 0.0 copy-start.2
  2.0 0.7 copy-done.2
  2.6 97.8 %shard_map.77 = (bf16[1024,512]{1,0:T(8,128)(2,1)S(1)}, bf16[1024,512]{1,0:T(8,128)(2,1)S(1)}) custom-call(bf16[64,8192]{1,0:T(8,128)(2,1)} %context_ref.1, bf16[1024,512]{1,0:T(8,128)(2,1)} %residual_ref.1, bf16[8192,512]{1,0:T(8,128)(2,1)} %weight_ref.1, f32[1,512]{1,0:T(1,128)S(1)} %bitcast.1, s32[16]{0:T(128)S(1)} %copy-done.1, s32[16]{0:T(128)S(1)} %copy-done.2), custom_call_target="tpu_custom_call" | custom-call | flops 8589934592 | bytes 12582912 | tf_op jit(solution)/shard_map/pallas_call | solution.py:286
  100.5 1.0 copy.10
  101.4 1.0 copy.11
Async XLA Ops:
  0.6 0.7 copy-start
  1.3 0.7 copy-start.1
  2.0 0.7 copy-start.2
